TPU v7x, 128 devices: a whole 4x4x4 slice. The times are simulated.
128 devices in a mesh: grp: 8 (over y, z_hi), lm: 16 (over x, z_lo, core).
Axes of the slice: x: 4, y: 4, z: 4 (z_hi: 2, z_lo: 2; z = z_hi * 2 + z_lo), core: 2. Of those that a mesh axis runs over, the one named last changes fastest.
Arguments:
- embeddings: bfloat16 [32768, 512], P(('grp', 'lm')), may hold values from -14 to 14
- landmarks: bfloat16 [32768, 512], P('lm'), may hold values from -14 to 14
- start_vectors: float32 [32768, 128], P(('grp', 'lm')), may hold values from -10 to 10
- row_weight: float32 [32768], P(('grp', 'lm')), may hold values from 0.1 to 9
- spread: float32 [1], replicated, may hold values from 11.313708 to 33.941124
Outputs:
- subspace: float32 [32768, 128], P(('grp', 'lm'))
All inputs are finite; a program needn't handle non-finite values.
Results may differ from a plain program's by a relative error of at most 0.019.
Values may be sent and summed in bfloat16 or wider, within the bound.
No kernel may reach another device: no remote copies, remote signals or barrier semaphores. Data moves between devices by JAX's collectives and lax.ppermute only.
A program may use at most 128 MiB of HBM per device.

v0:
```python
import jax
import jax.numpy as jnp
from jax import lax
from jax.sharding import PartitionSpec as P

ITERS = 2


def unit_rows(values):
    values = values.astype(jnp.float32)
    scale = lax.rsqrt(jnp.sum(values * values, axis=1, keepdims=True) + 1e-06)
    return (values * scale).astype(jnp.bfloat16)


def kernel_values(rows_unit, marks_unit, gamma):
    cosine = jnp.einsum("rd,ld->rl", rows_unit, marks_unit, preferred_element_type=jnp.float32)
    return jnp.exp(gamma * cosine)


def local(embeddings, landmarks, start_vectors, row_weight, spread):
    own_rows = embeddings.shape[0]
    marks = landmarks.shape[0]
    groups = lax.axis_size("grp")
    members = lax.axis_size("lm")
    total_rows = own_rows * groups * members
    group_rows = own_rows * members
    gamma = spread[0]
    rows_unit = unit_rows(embeddings)
    marks_unit = unit_rows(landmarks)
    sums = jnp.zeros((marks,), jnp.float32)
    weights = jnp.zeros((group_rows,), jnp.float32)
    part_rows = lax.all_gather(rows_unit, "lm", axis=0, tiled=True)
    part_weight = lax.all_gather(row_weight.astype(jnp.bfloat16), "lm", axis=0, tiled=True).astype(
        jnp.float32
    )
    values = kernel_values(part_rows, marks_unit, gamma)
    build_tile = values.astype(jnp.bfloat16)
    weights = lax.dynamic_update_slice_in_dim(weights, part_weight, jnp.int32(0), 0)
    sums = sums + jnp.sum(part_weight[:, None] * values, axis=0)
    mean_sum, weight_sum = lax.psum((sums, jnp.sum(weights)), "grp")
    means = mean_sum / weight_sum
    vectors = start_vectors
    weighted_full = row_weight[:, None] * vectors
    totals = lax.psum(jnp.sum(weighted_full, axis=0), ("grp", "lm"))
    group_weighted = lax.all_gather(weighted_full.astype(jnp.bfloat16), "lm", axis=0, tiled=True)
    for step in range(ITERS):
        side = (
            lax.psum(
                jnp.einsum(
                    "rl,rv->lv", build_tile, group_weighted, preferred_element_type=jnp.float32
                ),
                "grp",
            )
            - means[:, None] * totals[None, :]
        )
        side_b = side.astype(jnp.bfloat16)
        shift = jnp.dot(means, side_b.astype(jnp.float32), precision=lax.Precision.HIGHEST)
        image = lax.psum_scatter(
            weights[:, None]
            * (jnp.dot(build_tile, side_b, preferred_element_type=jnp.float32) - shift[None, :]),
            "lm",
            scatter_dimension=0,
            tiled=True,
        )
        square, column = lax.psum(
            (jnp.sum(image * image, axis=0), jnp.sum(row_weight[:, None] * image, axis=0)),
            ("grp", "lm"),
        )
        scale = jnp.sqrt(square / total_rows + 1e-06)
        vectors = image / scale[None, :]
        totals = column / scale
        if step + 1 < ITERS:
            group_weighted = lax.all_gather(
                (row_weight[:, None] * vectors).astype(jnp.bfloat16), "lm", axis=0, tiled=True
            )
    return vectors


def solution(mesh):
    in_specs = (
        P(("grp", "lm"), None),
        P("lm", None),
        P(("grp", "lm"), None),
        P(("grp", "lm")),
        P(),
    )
    out_specs = P(("grp", "lm"), None)
    return jax.shard_map(local, mesh=mesh, in_specs=in_specs, out_specs=out_specs, check_vma=False)
```

profile of v0, /device:TPU:1, one launch (start us, length us, event | category | flops | bytes accessed | tf_op | source)
XLA Modules:
  0.0 612.0 jit_solution(1574066524591326856)
XLA Ops:
  6.5 1.1 fusion.8
  7.6 1.8 fusion.9
  9.5 1.6 multiply_reduce_fusion.4
  11.2 2.1 fusion.3
  14.0 21.3 %all-gather = bf16[16,1,256]{2,1,0:T(2,128)(2,1)S(1)} all-gather(bf16[1,1,256]{2,1,0:T(2,128)(2,1)S(1)} %reshape.21), channel_id=1, replica_groups=mesh['grp'=8,'lm'=16] {'lm'}, dimensions={0}, use_global_device_ids=true | all-gather | bytes 8704 | tf_op jit(solution)/shard_map/all_gather | solution.py:33
  36.0 14.6 %all-gather.5.cloned.1.call-done = bf16[4096,512]{1,0:T(8,128)(2,1)} async-done(((bf16[256,512]{1,0:T(8,128)(2,1)}), bf16[4096,512]{1,0:T(8,128)(2,1)}) %all-gather.5.cloned.1.call-update) | async-done | bytes 4194320 | tf_op jit(solution)/shard_map/all_gather | solution.py:32
  50.6 16.2 %multiply_reduce_fusion = (f32[2048]{0:T(1024)S(1)}, bf16[4096,2048]{1,0:T(8,128)(2,1)}) fusion(f32[4096]{0:T(1024)S(1)} %bitcast.20, f32[]{:T(128)} %bitcast.17, bf16[4096,512]{1,0:T(8,128)(2,1)} %all-gather.5.cloned.1.call-done, bf16[2048,512]{1,0:T(8,128)(2,1)} %param.6, f32[2048]{0:T(1024)S(1)} %add_rsqrt_fusion), kind=kOutput, calls=%fused_computation | convolution fusion | flops 8626632704 | bytes 23101444 | tf_op jit(solution)/shard_map/rd,ld->rl/dot_general | solution.py:16
  66.7 18.1 %all-gather.7.cloned.1.call-done = bf16[4096,128]{1,0:T(8,128)(2,1)} async-done(((bf16[256,128]{1,0:T(8,128)(2,1)}), bf16[4096,128]{1,0:T(8,128)(2,1)}) %all-gather.7.cloned.1.call-update) | async-done | bytes 1048592 | tf_op jit(solution)/shard_map/all_gather | solution.py:45
  84.8 11.6 %fusion.11 = f32[2048,128]{1,0:T(8,128)} fusion(bf16[4096,2048]{1,0:T(8,128)(2,1)} %get-tuple-element.12, bf16[4096,128]{1,0:T(8,128)(2,1)} %all-gather.7.cloned.1.call-done), kind=kOutput, calls=%fused_computation.35 | convolution fusion | flops 2147483648 | bytes 18874368 | tf_op jit(solution)/shard_map/rl,rv->lv/dot_general | solution.py:49
  96.5 69.1 %psum.59 = f32[128]{0:T(128)S(1)} all-reduce(f32[128]{0:T(128)S(1)} %get-tuple-element.13), channel_id=1, replica_groups=mesh['grp'=8,'lm'=16] {'grp','lm'}, use_global_device_ids=true, to_apply=%region_8.0 | all-reduce | flops 128 | bytes 1024 | tf_op jit(solution)/shard_map/psum | solution.py:44
  166.3 19.9 %all-reduce.1 = (f32[2048]{0:T(1024)S(1)}, f32[]{:T(128)}) all-reduce(f32[2048]{0:T(1024)S(1)} %get-tuple-element.11, f32[]{:T(128)} %convert_reduce_fusion), channel_id=1, replica_groups=mesh['grp'=8,'lm'=16] {'grp'}, use_global_device_ids=true, to_apply=%region_4.0 | all-reduce | flops 2049 | bytes 16392 | tf_op jit(solution)/shard_map/psum | solution.py:40
  186.9 1.8 convolution_bitcast_fusion.1
  188.7 12.0 %fusion.2 = f32[4096,128]{1,0:T(8,128)} fusion(bf16[4096,2048]{1,0:T(8,128)(2,1)} %get-tuple-element.12, f32[128]{0:T(128)S(1)} %convolution_bitcast_fusion.1, f32[4096]{0:T(1024)S(1)} %bitcast.21, f32[2048,128]{1,0:T(8,128)} %all-reduce.5.cloned.1.call-done, f32[128]{0:T(128)S(1)} %psum.59, f32[2048]{0:T(1024)S(1)} %broadcast_divide_fusion.1), kind=kOutput, calls=%fused_computation.8 | convolution fusion | flops 2149318656 | bytes 19948544 | tf_op jit(solution)/shard_map/dot_general | solution.py:60
  200.7 61.7 %reduce-scatter.3.cloned.1.call-done = f32[256,128]{1,0:T(8,128)} async-done(((f32[4096,128]{1,0:T(8,128)}), f32[256,128]{1,0:T(8,128)}) %reduce-scatter.3.cloned.1.call-update) | async-done | bytes 131088 | tf_op jit(solution)/shard_map/reduce_scatter | solution.py:58
  263.5 67.6 %all-reduce = (f32[128]{0:T(128)S(1)}, f32[128]{0:T(128)S(1)}) all-reduce(f32[128]{0:T(128)S(1)} %get-tuple-element.6, f32[128]{0:T(128)S(1)} %get-tuple-element.5), channel_id=1, replica_groups=mesh['grp'=8,'lm'=16] {'grp','lm'}, use_global_device_ids=true, to_apply=%region_11.0 | all-reduce | flops 256 | bytes 2048 | tf_op jit(solution)/shard_map/psum | solution.py:65
  331.1 1.6 multiply_convert_fusion
  333.1 29.2 %all-gather.9.cloned.1.call-done = bf16[4096,128]{1,0:T(8,128)(2,1)} async-done(((bf16[256,128]{1,0:T(8,128)(2,1)}), bf16[4096,128]{1,0:T(8,128)(2,1)}) %all-gather.9.cloned.1.call-update) | async-done | bytes 1048592 | tf_op jit(solution)/shard_map/all_gather | solution.py:73
  362.2 11.6 %fusion.12 = f32[2048,128]{1,0:T(8,128)} fusion(bf16[4096,2048]{1,0:T(8,128)(2,1)} %get-tuple-element.12, bf16[4096,128]{1,0:T(8,128)(2,1)} %all-gather.9.cloned.1.call-done), kind=kOutput, calls=%fused_computation.36 | convolution fusion | flops 2147483648 | bytes 18874368 | tf_op jit(solution)/shard_map/rl,rv->lv/dot_general | solution.py:49
  373.9 83.7 %all-reduce.7.cloned.1.call-done = f32[2048,128]{1,0:T(8,128)} async-done(((f32[2048,128]{1,0:T(8,128)}), f32[2048,128]{1,0:T(8,128)}) %all-reduce.7.cloned.1.call-update) | async-done | bytes 1048592 | tf_op jit(solution)/shard_map/psum | solution.py:48
  457.6 1.8 convolution_bitcast_fusion
  459.4 12.0 %fusion.1 = f32[4096,128]{1,0:T(8,128)} fusion(bf16[4096,2048]{1,0:T(8,128)(2,1)} %get-tuple-element.12, f32[128]{0:T(128)S(1)} %convolution_bitcast_fusion, f32[4096]{0:T(1024)S(1)} %bitcast.22, f32[2048,128]{1,0:T(8,128)} %all-reduce.7.cloned.1.call-done, f32[128]{0:T(128)S(1)} %get-tuple-element.15, f32[2048]{0:T(1024)S(1)} %broadcast_divide_fusion.1), kind=kOutput, calls=%fused_computation.6 | convolution fusion | flops 2149318656 | bytes 19948544 | tf_op jit(solution)/shard_map/dot_general | solution.py:60
  471.4 63.1 %reduce-scatter.5.cloned.1.call-done = f32[256,128]{1,0:T(8,128)} async-done(((f32[4096,128]{1,0:T(8,128)}), f32[256,128]{1,0:T(8,128)}) %reduce-scatter.5.cloned.1.call-update) | async-done | bytes 131088 | tf_op jit(solution)/shard_map/reduce_scatter | solution.py:58
  535.4 68.2 %psum.63 = f32[128]{0:T(128)S(1)} all-reduce(f32[128]{0:T(128)S(1)} %multiply_reduce_fusion.1), channel_id=1, replica_groups=mesh['grp'=8,'lm'=16] {'grp','lm'}, use_global_device_ids=true, to_apply=%region_17.0 | all-reduce | flops 128 | bytes 1024 | tf_op jit(solution)/shard_map/psum | solution.py:65
  603.6 1.6 broadcast_divide_fusion
  (28 shorter events, 4.6 us)
Async XLA Ops:
  6.5 44.0 %all-gather.5.cloned.1.call-start = ((), (), s32[]{:S(2)}) async-start(), calls=%async_computation.2 | async-start | bytes 4456448 | tf_op jit(solution)/shard_map/all_gather | solution.py:32
  9.4 75.4 %all-gather.7.cloned.1.call-start = ((), (), s32[]{:S(2)}) async-start(), calls=%async_computation.3 | async-start | bytes 1114112 | tf_op jit(solution)/shard_map/all_gather | solution.py:45
  11.1 175.7 %all-reduce.5.cloned.1.call-start = ((), (), s32[]{:S(2)}) async-start(), calls=%async_computation.4 | async-start | bytes 2097152 | tf_op jit(solution)/shard_map/psum | solution.py:48
  96.5 166.0 %reduce-scatter.3.cloned.1.call-start = ((), (), s32[]{:S(2)}) async-start(), calls=%async_computation.5 | async-start | bytes 2228224 | tf_op jit(solution)/shard_map/reduce_scatter | solution.py:58
  188.7 73.8 %copy-start = (f32[256]{0:T(256)S(1)}, f32[256]{0:T(256)}, u32[]{:S(2)}) copy-start(f32[256]{0:T(256)} %param.8) | copy-start | bytes 3076
  200.7 161.5 %all-gather.9.cloned.1.call-start = ((), (), s32[]{:S(2)}) async-start(), calls=%async_computation.6 | async-start | bytes 1114112 | tf_op jit(solution)/shard_map/all_gather | solution.py:73
  332.8 124.8 %all-reduce.7.cloned.1.call-start = ((), (), s32[]{:S(2)}) async-start(), calls=%async_computation.7 | async-start | bytes 2097152 | tf_op jit(solution)/shard_map/psum | solution.py:48
  373.9 160.6 %reduce-scatter.5.cloned.1.call-start = ((), (), s32[]{:S(2)}) async-start(), calls=%async_computation.8 | async-start | bytes 2228224 | tf_op jit(solution)/shard_map/reduce_scatter | solution.py:58
Sparse Core Ops, SparseCore 0:
  9.5 40.9 all-gather.4
  52.3 32.5 all-gather.6
  96.6 84.5 all-reduce.4
  200.8 61.5 reduce-scatter.2
  332.9 29.2 all-gather.8
  374.0 83.5 all-reduce.6
  471.5 62.8 reduce-scatter.4
where the time goes:
time: 613 us; the launch traced here: 612 us
  waiting for transfers between devices  270 us (44%)
  blocking collectives  246 us (40%)
  matrix products  67 us (11%)
  between operations  14.2 us (2%)
  other arithmetic  13.8 us (2%)
    psum x2, blocking collectives, local(): lax.psum((jnp.sum(image * image, axis=0), jnp.sum(row_weight[:, None] * i...  136 us
    reduce_scatter x2, waiting for transfers between devices, local(): lax.psum_scatter(weights[:, None] * (jnp.dot(build_tile, side_b, preferre...  125 us
    psum x2, waiting for transfers between devices, local(): lax.psum(jnp.einsum('rl,rv->lv', build_tile, group_weighted, preferred_el...  83.7 us
    psum x1, blocking collectives, local(): totals = lax.psum(jnp.sum(weighted_full, axis=0), ('grp', 'lm'))  69.1 us
    all_gather x1, waiting for transfers between devices, local(): lax.all_gather((row_weight[:, None] * vectors).astype(jnp.bfloat16), 'lm'...  29.2 us
    dot_general x2, matrix products, local(): jnp.dot(build_tile, side_b, preferred_element_type=jnp.float32)  24 us
    dot_general x2, matrix products, local(): jnp.einsum('rl,rv->lv', build_tile, group_weighted, preferred_element_typ...  23.2 us
    all_gather x1, blocking collectives, local(): lax.all_gather(row_weight.astype(jnp.bfloat16), 'lm', axis=0, tiled=True)  21.3 us
  transfers between devices with their start and end apart: 7, of which 6 were waited for; matrix products, arithmetic and copies ran while one was open for 4% of the time, Pallas kernels for 0%

commit v1 on v0

--- a/solution.py
+++ b/solution.py
@@ -45,11 +45,14 @@
     group_weighted = lax.all_gather(weighted_full.astype(jnp.bfloat16), "lm", axis=0, tiled=True)
     for step in range(ITERS):
         side = (
-            lax.psum(
-                jnp.einsum(
-                    "rl,rv->lv", build_tile, group_weighted, preferred_element_type=jnp.float32
+            jnp.sum(
+                lax.all_gather(
+                    jnp.einsum(
+                        "rl,rv->lv", build_tile, group_weighted, preferred_element_type=jnp.float32
+                    ),
+                    "grp",
                 ),
-                "grp",
+                axis=0,
             )
             - means[:, None] * totals[None, :]
         )

time: 613 us -> 665 us (1.085)
  blocking collectives: 246 us -> 274 us
  waiting for transfers between devices: 270 us -> 291 us
  other arithmetic: 13.8 us -> 21.6 us
    all_gather x0 -> x2, waiting for transfers between devices: none -> 108 us  [local(): lax.all_gather(jnp.einsum('rl,rv->lv', build_tile, group_weighted, prefer...]
    psum x2 -> x0, waiting for transfers between devices: 83.7 us -> none  [local(): lax.psum(jnp.einsum('rl,rv->lv', build_tile, group_weighted, preferred_el...]
    psum x1, blocking collectives: 69.1 us -> 98.7 us  [local(): totals = lax.psum(jnp.sum(weighted_full, axis=0), ('grp', 'lm'))]
    reduce_sum x0 -> x2, other arithmetic: none -> 7.8 us  [local(): jnp.sum(lax.all_gather(jnp.einsum('rl,rv->lv', build_tile, group_weighted...]
  transfers between devices with their start and end apart: 7 -> 7, of which waited for: 6 -> 6; matrix products, arithmetic and copies ran while one was open for 4% -> 3% of each run, Pallas kernels for 0% -> 0%
where the time goes in v1:
time: 665 us
  waiting for transfers between devices  291 us (44%)
  blocking collectives  274 us (41%)
  matrix products  64.2 us (10%)
  other arithmetic  21.6 us (3%)
  between operations  14.2 us (2%)
    psum x2, blocking collectives, local(): lax.psum((jnp.sum(image * image, axis=0), jnp.sum(row_weight[:, None] * i...  136 us
    reduce_scatter x2, waiting for transfers between devices, local(): lax.psum_scatter(weights[:, None] * (jnp.dot(build_tile, side_b, preferre...  120 us
    all_gather x2, waiting for transfers between devices, local(): lax.all_gather(jnp.einsum('rl,rv->lv', build_tile, group_weighted, prefer...  108 us
    psum x1, blocking collectives, local(): totals = lax.psum(jnp.sum(weighted_full, axis=0), ('grp', 'lm'))  98.7 us
    all_gather x1, waiting for transfers between devices, local(): lax.all_gather((row_weight[:, None] * vectors).astype(jnp.bfloat16), 'lm'...  29.2 us
    dot_general x2, matrix products, local(): jnp.dot(build_tile, side_b, preferred_element_type=jnp.float32)  23.6 us
    dot_general x2, matrix products, local(): jnp.einsum('rl,rv->lv', build_tile, group_weighted, preferred_element_typ...  23.4 us
    all_gather x1, blocking collectives, local(): lax.all_gather(row_weight.astype(jnp.bfloat16), 'lm', axis=0, tiled=True)  21.4 us
  transfers between devices with their start and end apart: 7, of which 6 were waited for; matrix products, arithmetic and copies ran while one was open for 3% of the time, Pallas kernels for 0%

profile of v1, /device:TPU:1, one launch (start us, length us, event | category | flops | bytes accessed | tf_op | source)
XLA Modules:
  0.0 664.8 jit_solution(5445728159958721024)
XLA Ops:
  6.5 1.1 fusion.8
  7.6 1.8 fusion.9
  9.5 1.6 multiply_reduce_fusion.4
  11.2 2.1 fusion.3
  14.6 21.4 %all-gather.2 = bf16[16,1,256]{2,1,0:T(2,128)(2,1)S(1)} all-gather(bf16[1,1,256]{2,1,0:T(2,128)(2,1)S(1)} %reshape.23), channel_id=1, replica_groups=mesh['grp'=8,'lm'=16] {'lm'}, dimensions={0}, use_global_device_ids=true | all-gather | bytes 8704 | tf_op jit(solution)/shard_map/all_gather | solution.py:33
  36.0 14.6 %all-gather.9.cloned.1.call-done = bf16[4096,512]{1,0:T(8,128)(2,1)} async-done(((bf16[256,512]{1,0:T(8,128)(2,1)}), bf16[4096,512]{1,0:T(8,128)(2,1)}) %all-gather.9.cloned.1.call-update) | async-done | bytes 4194320 | tf_op jit(solution)/shard_map/all_gather | solution.py:32
  50.6 16.2 %multiply_reduce_fusion = (f32[2048]{0:T(1024)S(1)}, bf16[4096,2048]{1,0:T(8,128)(2,1)}) fusion(f32[4096]{0:T(1024)S(1)} %bitcast.24, f32[]{:T(128)} %bitcast.19, bf16[4096,512]{1,0:T(8,128)(2,1)} %all-gather.9.cloned.1.call-done, bf16[2048,512]{1,0:T(8,128)(2,1)} %param.6, f32[2048]{0:T(1024)S(1)} %add_rsqrt_fusion), kind=kOutput, calls=%fused_computation | convolution fusion | flops 8626632704 | bytes 23101444 | tf_op jit(solution)/shard_map/rd,ld->rl/dot_general | solution.py:16
  66.8 18.0 %all-gather.11.cloned.1.call-done = bf16[4096,128]{1,0:T(8,128)(2,1)} async-done(((bf16[256,128]{1,0:T(8,128)(2,1)}), bf16[4096,128]{1,0:T(8,128)(2,1)}) %all-gather.11.cloned.1.call-update) | async-done | bytes 1048592 | tf_op jit(solution)/shard_map/all_gather | solution.py:45
  84.8 11.7 %fusion.11 = f32[2048,128]{1,0:T(8,128)} fusion(bf16[4096,2048]{1,0:T(8,128)(2,1)} %get-tuple-element.12, bf16[4096,128]{1,0:T(8,128)(2,1)} %all-gather.11.cloned.1.call-done), kind=kOutput, calls=%fused_computation.35 | convolution fusion | flops 2147483648 | bytes 18874368 | tf_op jit(solution)/shard_map/rl,rv->lv/dot_general | solution.py:50
  96.6 98.7 %psum.44 = f32[128]{0:T(128)S(1)} all-reduce(f32[128]{0:T(128)S(1)} %get-tuple-element.13), channel_id=1, replica_groups=mesh['grp'=8,'lm'=16] {'grp','lm'}, use_global_device_ids=true, to_apply=%region_8.0 | all-reduce | flops 128 | bytes 1024 | tf_op jit(solution)/shard_map/psum | solution.py:44
  196.0 17.4 %all-reduce.1 = (f32[2048]{0:T(1024)S(1)}, f32[]{:T(128)}) all-reduce(f32[2048]{0:T(1024)S(1)} %get-tuple-element.11, f32[]{:T(128)} %convert_reduce_fusion), channel_id=1, replica_groups=mesh['grp'=8,'lm'=16] {'grp'}, use_global_device_ids=true, to_apply=%region_4.0 | all-reduce | flops 2049 | bytes 16392 | tf_op jit(solution)/shard_map/psum | solution.py:40
  214.0 3.9 reduce_sum.92
  218.5 11.8 %fusion.2 = f32[4096,128]{1,0:T(8,128)} fusion(bf16[4096,2048]{1,0:T(8,128)(2,1)} %get-tuple-element.12, f32[128]{0:T(128)S(1)} %convolution_bitcast_fusion.1, f32[4096]{0:T(1024)S(1)} %bitcast.25, f32[2048,128]{1,0:T(8,128)S(1)} %reduce_sum.92, f32[128]{0:T(128)S(1)} %psum.44, f32[2048]{0:T(1024)S(1)} %broadcast_divide_fusion.1), kind=kOutput, calls=%fused_computation.8 | convolution fusion | flops 2149318656 | bytes 19948544 | tf_op jit(solution)/shard_map/dot_general | solution.py:63
  230.4 61.9 %reduce-scatter.3.cloned.1.call-done = f32[256,128]{1,0:T(8,128)} async-done(((f32[4096,128]{1,0:T(8,128)}), f32[256,128]{1,0:T(8,128)}) %reduce-scatter.3.cloned.1.call-update) | async-done | bytes 131088 | tf_op jit(solution)/shard_map/reduce_scatter | solution.py:61
  293.4 68.0 %all-reduce = (f32[128]{0:T(128)S(1)}, f32[128]{0:T(128)S(1)}) all-reduce(f32[128]{0:T(128)S(1)} %get-tuple-element.6, f32[128]{0:T(128)S(1)} %get-tuple-element.5), channel_id=1, replica_groups=mesh['grp'=8,'lm'=16] {'grp','lm'}, use_global_device_ids=true, to_apply=%region_11.0 | all-reduce | flops 256 | bytes 2048 | tf_op jit(solution)/shard_map/psum | solution.py:68
  361.4 1.6 multiply_convert_fusion
  363.3 29.2 %all-gather.13.cloned.1.call-done = bf16[4096,128]{1,0:T(8,128)(2,1)} async-done(((bf16[256,128]{1,0:T(8,128)(2,1)}), bf16[4096,128]{1,0:T(8,128)(2,1)}) %all-gather.13.cloned.1.call-update) | async-done | bytes 1048592 | tf_op jit(solution)/shard_map/all_gather | solution.py:76
  392.5 11.7 %fusion.12 = f32[2048,128]{1,0:T(8,128)} fusion(bf16[4096,2048]{1,0:T(8,128)(2,1)} %get-tuple-element.12, bf16[4096,128]{1,0:T(8,128)(2,1)} %all-gather.13.cloned.1.call-done), kind=kOutput, calls=%fused_computation.36 | convolution fusion | flops 2147483648 | bytes 18874368 | tf_op jit(solution)/shard_map/rl,rv->lv/dot_general | solution.py:50
  404.2 108.3 %all-gather.17.cloned.1.call-done = f32[16384,128]{1,0:T(8,128)} async-done(((f32[2048,128]{1,0:T(8,128)}), f32[16384,128]{1,0:T(8,128)}) %all-gather.17.cloned.1.call-update) | async-done | bytes 8388624 | tf_op jit(solution)/shard_map/all_gather | solution.py:49
  512.6 3.9 reduce_sum.97
  517.0 11.8 %fusion.1 = f32[4096,128]{1,0:T(8,128)} fusion(bf16[4096,2048]{1,0:T(8,128)(2,1)} %get-tuple-element.12, f32[128]{0:T(128)S(1)} %convolution_bitcast_fusion, f32[4096]{0:T(1024)S(1)} %bitcast.26, f32[2048,128]{1,0:T(8,128)S(1)} %reduce_sum.97, f32[128]{0:T(128)S(1)} %get-tuple-element.15, f32[2048]{0:T(1024)S(1)} %broadcast_divide_fusion.1), kind=kOutput, calls=%fused_computation.6 | convolution fusion | flops 2149318656 | bytes 19948544 | tf_op jit(solution)/shard_map/dot_general | solution.py:63
  528.8 58.4 %reduce-scatter.5.cloned.1.call-done = f32[256,128]{1,0:T(8,128)} async-done(((f32[4096,128]{1,0:T(8,128)}), f32[256,128]{1,0:T(8,128)}) %reduce-scatter.5.cloned.1.call-update) | async-done | bytes 131088 | tf_op jit(solution)/shard_map/reduce_scatter | solution.py:61
  588.2 68.1 %psum.47 = f32[128]{0:T(128)S(1)} all-reduce(f32[128]{0:T(128)S(1)} %multiply_reduce_fusion.1), channel_id=1, replica_groups=mesh['grp'=8,'lm'=16] {'grp','lm'}, use_global_device_ids=true, to_apply=%region_17.0 | all-reduce | flops 128 | bytes 1024 | tf_op jit(solution)/shard_map/psum | solution.py:68
  656.3 1.6 broadcast_divide_fusion
  (30 shorter events, 5.7 us)
Async XLA Ops:
  6.5 44.1 %all-gather.9.cloned.1.call-start = ((), (), s32[]{:S(2)}) async-start(), calls=%async_computation.2 | async-start | bytes 4456448 | tf_op jit(solution)/shard_map/all_gather | solution.py:32
  9.4 75.4 %all-gather.11.cloned.1.call-start = ((), (), s32[]{:S(2)}) async-start(), calls=%async_computation.3 | async-start | bytes 1114112 | tf_op jit(solution)/shard_map/all_gather | solution.py:45
  11.1 202.9 %all-gather.15.cloned.1.call-start = ((), (), s32[]{:S(2)}) async-start(), calls=%async_computation.7 | async-start | bytes 9437184 | tf_op jit(solution)/shard_map/all_gather | solution.py:49
  96.5 195.8 %reduce-scatter.3.cloned.1.call-start = ((), (), s32[]{:S(2)}) async-start(), calls=%async_computation.4 | async-start | bytes 2228224 | tf_op jit(solution)/shard_map/reduce_scatter | solution.py:61
  218.5 73.8 %copy-start = (f32[256]{0:T(256)S(1)}, f32[256]{0:T(256)}, u32[]{:S(2)}) copy-start(f32[256]{0:T(256)} %param.8) | copy-start | bytes 3076
  230.3 162.1 %all-gather.13.cloned.1.call-start = ((), (), s32[]{:S(2)}) async-start(), calls=%async_computation.5 | async-start | bytes 1114112 | tf_op jit(solution)/shard_map/all_gather | solution.py:76
  363.1 149.5 %all-gather.17.cloned.1.call-start = ((), (), s32[]{:S(2)}) async-start(), calls=%async_computation.8 | async-start | bytes 9437184 | tf_op jit(solution)/shard_map/all_gather | solution.py:49
  404.2 183.0 %reduce-scatter.5.cloned.1.call-start = ((), (), s32[]{:S(2)}) async-start(), calls=%async_computation.6 | async-start | bytes 2228224 | tf_op jit(solution)/shard_map/reduce_scatter | solution.py:61
Sparse Core Ops, SparseCore 0:
  9.5 41.0 all-gather.8
  52.3 32.4 all-gather.10
  96.7 109.5 all-gather.14
  230.5 61.8 reduce-scatter.2
  363.2 29.2 all-gather.12
  404.3 108.1 all-gather.16
  529.0 58.2 reduce-scatter.4
